TPU v7x, 32 devices: a whole 2x2x4 slice. The times are simulated.
32 devices in a mesh: tensor: 2 (over x), context: 16 (over z, y, core).
Axes of the slice: x: 2, y: 2, z: 4, core: 2. Of those that a mesh axis runs over, the one named last changes fastest.
Arguments:
- q_proj: bfloat16 [4096, 8192], P('context', 'tensor'), may hold values from -6 to 6
- k_proj: bfloat16 [4096, 8192], P('context', 'tensor'), may hold values from -6 to 6
- v_proj: bfloat16 [4096, 8192], P('context', 'tensor'), may hold values from -6 to 6
- short_filter: bfloat16 [3, 3, 512], P(None, None, 'tensor'), may hold values from -3.5 to 3.5
- residue: float32 [16, 8192], P(None, 'tensor'), may hold values from -1.5 to 1.5
- decay_rate: float32 [16, 8192], P(None, 'tensor'), may hold values from 0.5 to 128
- out_weight: bfloat16 [4096, 8192], P('context', 'tensor'), may hold values from -0.0625 to 0.0625
Outputs:
- projected: bfloat16 [4096, 4096], P('tensor', 'context')
All inputs are finite; a program needn't handle non-finite values.
Results may differ from a plain program's by a relative error of at most 0.02.
Values may be sent and summed in bfloat16 or wider, within the bound.
No kernel may reach another device: no remote copies, remote signals or barrier semaphores. Data moves between devices by JAX's collectives and lax.ppermute only.
A program may use at most 256 MiB of HBM per device.

v0:
```python
import jax
import jax.numpy as jnp
import numpy as np
from jax import lax
from jax.sharding import PartitionSpec as P


def passed_along(block, axis, distance):
    devices = range(lax.axis_size(axis))
    route = [(i - distance, i) for i in devices if i - distance in devices]
    return lax.ppermute(block, axis, route)


def prefix(part, axis, combine, identity):
    place = lax.axis_index(axis)
    gathered = jax.tree.map(lambda a: lax.all_gather(a, axis), part)
    state = jax.tree.map(lambda a, e: jnp.zeros_like(a) + jnp.asarray(e, a.dtype), part, identity)

    def one(lap, state):
        return combine(
            state, jax.tree.map(lambda a: lax.dynamic_index_in_dim(a, lap, 0, False), gathered)
        )

    return lax.fori_loop(0, place, one, state)


def short_pass(extended, filters, group_width):
    tap_count = filters.shape[0]
    length_rows, chan_count = extended.shape
    groups = filters.shape[1]
    widened = jnp.broadcast_to(
        filters.astype(jnp.float32)[:, :, None], (tap_count, groups, group_width)
    ).reshape(tap_count, chan_count)
    out_rows = length_rows - tap_count + 1
    running = jnp.zeros((out_rows, chan_count), jnp.float32)
    for offset in range(tap_count):
        begin = tap_count - 1 - offset
        running = running + widened[offset][None, :] * extended[begin : begin + out_rows].astype(
            jnp.float32
        )
    return running


def compose(earlier, later):
    return (earlier[0] * later[0], earlier[1] * later[0] + later[1])


def per_device(q_proj, k_proj, v_proj, short_filter, residue, decay_rate, out_weight):
    row_count, chan_count = q_proj.shape
    short_taps = short_filter.shape[1]
    group_width = chan_count // short_filter.shape[2]
    lead_rows = short_taps - 1
    q_rim, k_rim, v_rim = passed_along(
        (
            q_proj[row_count - lead_rows :],
            k_proj[row_count - lead_rows :],
            v_proj[row_count - lead_rows :],
        ),
        "context",
        1,
    )
    q_feat = short_pass(
        jnp.concatenate([q_rim, q_proj], axis=0), short_filter[0], group_width
    ).astype(jnp.bfloat16)
    k_feat = short_pass(
        jnp.concatenate([k_rim, k_proj], axis=0), short_filter[1], group_width
    ).astype(jnp.bfloat16)
    v_feat = short_pass(
        jnp.concatenate([v_rim, v_proj], axis=0), short_filter[2], group_width
    ).astype(jnp.bfloat16)
    product = (k_feat.astype(jnp.float32) * v_feat.astype(jnp.float32)).astype(jnp.bfloat16)
    sub_len = 16
    sub_count = row_count // sub_len
    decay_step = decay_rate / (row_count * lax.axis_size("context"))
    mode_scale = residue * jnp.sqrt(2.0 * decay_step)
    offsets = jnp.arange(sub_len).astype(jnp.float32)
    intra_kernel = jnp.sum(
        mode_scale[None] * jnp.exp(-decay_step[None] * offsets[:, None, None]), axis=1
    )
    gap_table = np.arange(sub_len)[None, :] - np.arange(sub_len)[:, None]
    one_hot = (gap_table[:, :, None] == np.arange(sub_len)[None, None, :]).astype(np.float32)
    toeplitz = jnp.einsum(
        "sto,oc->stc", jnp.asarray(one_hot), intra_kernel, precision=lax.Precision.HIGHEST
    )
    local_rows = product.astype(jnp.float32).reshape(sub_count, sub_len, chan_count)
    local_part = jnp.einsum("qsc,stc->qtc", local_rows, toeplitz, precision=lax.Precision.HIGHEST)
    tail_powers = jnp.exp(-decay_step[None] * (sub_len - 1 - offsets)[:, None, None])
    sub_ends = jnp.einsum("qsc,smc->qmc", local_rows, tail_powers, precision=lax.Precision.HIGHEST)
    step_decay = jnp.broadcast_to(jnp.exp(-decay_step * sub_len)[None], sub_ends.shape)
    ignored, carried = lax.associative_scan(compose, (step_decay, sub_ends))
    block_state = carried[-1]
    previous = jnp.concatenate([jnp.zeros_like(carried[:1]), carried[:-1]], axis=0)
    block_decay = jnp.exp(-decay_step * row_count)
    unused, incoming = prefix(
        (block_decay, block_state),
        "context",
        compose,
        (jnp.ones_like(block_decay), jnp.zeros_like(block_state)),
    )
    start_decay = jnp.exp(
        -decay_step[None] * (sub_len * jnp.arange(sub_count)).astype(jnp.float32)[:, None, None]
    )
    prior = previous + start_decay * incoming[None]
    lead_powers = jnp.exp(-decay_step[None] * (offsets + 1.0)[:, None, None])
    carried_part = jnp.einsum(
        "qmc,smc->qsc", prior * mode_scale[None], lead_powers, precision=lax.Precision.HIGHEST
    )
    modal_out = (local_part + carried_part).reshape(row_count, chan_count)
    gated = (q_feat.astype(jnp.float32) * modal_out).astype(jnp.bfloat16)
    partial_terms = lax.dot_general(
        lax.all_gather(out_weight, "context", axis=0, tiled=True),
        gated,
        (((1,), (1,)), ((), ())),
        preferred_element_type=jnp.float32,
    )
    return lax.psum_scatter(
        partial_terms.astype(jnp.bfloat16), "tensor", scatter_dimension=0, tiled=True
    )


def solution(mesh):
    return jax.shard_map(
        per_device,
        mesh=mesh,
        in_specs=(
            P("context", "tensor"),
            P("context", "tensor"),
            P("context", "tensor"),
            P(None, None, "tensor"),
            P(None, "tensor"),
            P(None, "tensor"),
            P("context", "tensor"),
        ),
        out_specs=P("tensor", "context"),
        check_vma=False,
    )
```

profile of v0, /device:TPU:0, one launch (start us, length us, event | category | flops | bytes accessed | tf_op | source)
XLA Modules:
  0.0 470.4 jit_solution(9558431965637106797)
XLA Ops:
  6.5 0.9 slice.217
  7.4 2.4 collective-permute-start.1
  9.8 0.9 slice.227
  10.6 4.5 collective-permute-start.2
  15.2 2.0 sqrt_multiply_fusion
  17.3 0.8 slice_convert_fusion.2
  18.1 2.7 multiply_exponential_fusion
  22.1 18.0 %copy.86 = f32[16,16,4096]{1,0,2:T(8,128)} copy(f32[16,16,4096]{2,1,0:T(8,128)} %multiply_exponential_fusion) | data formatting | bytes 8388608 | tf_op jit(solution)/shard_map/exp | solution.py:87
  40.1 7.0 %multiply_convert_fusion = bf16[256,4096]{1,0:T(8,128)(2,1)S(1)} fusion(bf16[256,4096]{1,0:T(8,128)(2,1)} %param.11, bf16[2,4096]{1,0:T(2,128)(2,1)S(1)} %collective-permute-done.1, bf16[256,4096]{1,0:T(8,128)(2,1)} %param.12, bf16[2,4096]{1,0:T(2,128)(2,1)S(1)} %collective-permute-done.2, f32[4096]{0:T(1024)S(1)} %broadcast_in_dim.85, ...), kind=kLoop, calls=%fused_computation.10 | loop fusion | flops 35651584 | bytes 6422528 | tf_op jit(solution)/shard_map/convert_element_type | solution.py:71
  47.1 14.0 %copy.85 = bf16[16,16,4096]{1,0,2:T(8,128)(2,1)} copy(bf16[16,16,4096]{2,1,0:T(8,128)(2,1)S(1)} %bitcast.52) | data formatting | bytes 4194304 | tf_op jit(solution)/shard_map/reshape | solution.py:85
  61.0 35.8 %fusion.17 = f32[4096,16,16]{1,2,0:T(8,128)} fusion(f32[16,16,4096]{1,0,2:T(8,128)} %copy.86, bf16[16,16,4096]{1,0,2:T(8,128)(2,1)} %copy.85), kind=kOutput, calls=%fused_computation.65 | convolution fusion | flops 201326592 | bytes 10485760 | tf_op jit(solution)/shard_map/qsc,smc->qmc/dot_general | solution.py:88
  96.8 19.8 %copy.88 = f32[4096,16,16]{0,1,2:T(8,128)} copy(f32[4096,16,16]{1,2,0:T(8,128)} %fusion.17) | data formatting | bytes 8388608 | tf_op jit(solution)/shard_map/qsc,smc->qmc/dot_general | solution.py:88
  116.6 2.4 slice_add_fusion.1
  119.1 0.7 slice.274
  120.3 0.6 copy-done
  120.9 0.8 pad_maximum_fusion.5
  121.7 1.1 pad.28
  122.9 1.8 pad_add_fusion
  124.7 2.7 pad.29
  127.4 2.3 add.114
  129.7 4.7 %pad.31 = f32[8,16,4096]{2,1,0:T(8,128)} pad(f32[4,16,4096]{2,1,0:T(8,128)} %add.114, f32[]{:T(128)} %constant.12.clone.1), padding=1_0_1x0_0_0x0_0_0 | pad | bytes 3145732 | tf_op jit(solution)/shard_map/pad | solution.py:90
  134.4 1.3 fusion.6
  135.7 1.0 pad_maximum_fusion.4
  136.7 2.9 pad.30
  139.6 2.4 add.116
  142.0 4.9 %pad.122 = f32[15,16,4096]{2,1,0:T(8,128)} pad(f32[8,16,4096]{2,1,0:T(8,128)S(1)} %add.116, f32[]{:T(128)} %constant.12.clone.1), padding=0_0_1x0_0_0x0_0_0 | pad | bytes 6029316
  146.9 1.7 slice.359
  148.6 0.7 all-gather.7.cloned.1.call-update
  149.4 0.9 slice.207
  150.3 2.0 collective-permute-start
  153.0 1.0 slice.273
  153.9 5.0 %pad.33 = f32[16,16,4096]{2,1,0:T(8,128)} pad(f32[8,16,4096]{2,1,0:T(8,128)S(1)} %add.116, f32[]{:T(128)} %constant.12.clone.1), padding=1_0_1x0_0_0x0_0_0 | pad | bytes 6291460 | tf_op jit(solution)/shard_map/pad | solution.py:90
  159.0 3.0 fusion.5
  162.1 5.0 %pad.32 = f32[16,16,4096]{2,1,0:T(8,128)} pad(f32[8,16,4096]{2,1,0:T(8,128)S(1)} %pad_maximum_fusion.3, f32[]{:T(128)} %constant.12.clone.1), padding=0_1_1x0_0_0x0_0_0 | pad | bytes 6291460 | tf_op jit(solution)/shard_map/pad | solution.py:90
  167.0 5.7 %slice_add_fusion = f32[15,16,4096]{2,1,0:T(8,128)} fusion(f32[16,16,4096]{2,1,0:T(8,128)} %pad.33, f32[16,16,4096]{2,1,0:T(8,128)} %pad.32), kind=kLoop, calls=%fused_computation.15 | loop fusion | flops 983040 | bytes 11796480 | tf_op jit(solution)/shard_map/add | solution.py:90
  172.8 26.9 %all-gather.5.cloned.1.call-done = f32[16,16,4096]{2,1,0:T(8,128)} async-done(((f32[1,16,4096]{2,1,0:T(8,128)}), f32[16,16,4096]{2,1,0:T(8,128)}) %all-gather.5.cloned.1.call-update) | async-done | bytes 4194320 | tf_op jit(solution)/shard_map/all_gather | solution.py:16
  200.0 5.9 %multiply_reduce_fusion = (f32[16,4096]{1,0:T(8,128)S(1)}, f32[16,16,4096]{2,1,0:T(8,128)}, f32[16,16,4096]{2,1,0:T(8,128)}) fusion(f32[16]{0:T(128)S(1)} %get-tuple-element.99, f32[16,4096]{1,0:T(8,128)S(1)} %copy-done.3, f32[16,4096]{1,0:T(8,128)S(1)} %copy-done.9, f32[16,4096]{1,0:T(8,128)S(1)} %get-tuple-element.49, f32[16]{0:T(128)S(1)} %get-tuple-element.98, ...), kind=kLoop, calls=%fused_computation.13 | loop fusion | flops 8323072 | bytes 13369536 | tf_op jit(solution)/shard_map/reduce_sum | solution.py:77
  205.8 18.1 %copy.89 = f32[16,16,4096]{1,0,2:T(8,128)} copy(f32[16,16,4096]{2,1,0:T(8,128)} %get-tuple-element.76) | data formatting | bytes 8388608 | tf_op jit(solution)/shard_map/exp | solution.py:104
  223.9 17.9 %copy.90 = f32[16,16,4096]{1,0,2:T(8,128)} copy(f32[16,16,4096]{2,1,0:T(8,128)} %get-tuple-element.73) | data formatting | bytes 8388608 | tf_op jit(solution)/shard_map/mul | solution.py:106
  241.8 4.9 %fusion.10 = f32[16,16,4096]{2,1,0:T(8,128)} fusion(f32[16,16,16]{2,1,0:T(8,128)S(1)} %copy-done.10, f32[16,4096]{1,0:T(8,128)S(1)} %get-tuple-element.72), kind=kOutput, calls=%fused_computation.45 | convolution fusion | flops 201326592 | bytes 4472832 | tf_op jit(solution)/shard_map/sto,oc->stc/dot_general | solution.py:82
  246.7 18.0 %copy.84 = f32[16,16,4096]{0,1,2:T(8,128)} copy(f32[16,16,4096]{2,1,0:T(8,128)} %fusion.10) | data formatting | bytes 8388608 | tf_op jit(solution)/shard_map/sto,oc->stc/dot_general | solution.py:82
  264.7 61.0 %fusion.18 = f32[4096,16,16]{2,1,0:T(8,128)} fusion(f32[16,16,4096]{1,0,2:T(8,128)} %copy.89, f32[16,16,4096]{1,0,2:T(8,128)} %copy.90), kind=kOutput, calls=%fused_computation.66 | convolution fusion | flops 201326592 | bytes 12582912 | tf_op jit(solution)/shard_map/qmc,smc->qsc/dot_general | solution.py:105
  325.7 46.3 %add_bitcast_fusion = f32[16,16,4096]{0,1,2:T(8,128)} fusion(f32[4096,16,16]{2,1,0:T(8,128)} %fusion.18, f32[16,16,4096]{0,1,2:T(8,128)} %copy.84, bf16[16,16,4096]{1,0,2:T(8,128)(2,1)} %copy.85), kind=kOutput, calls=%fused_computation.2 | convolution fusion | flops 202375168 | bytes 14680064 | tf_op jit(solution)/shard_map/qsc,stc->qtc/dot_general | solution.py:86
  372.0 19.9 %copy.91 = f32[16,16,4096]{2,1,0:T(8,128)} copy(f32[16,16,4096]{0,1,2:T(8,128)} %add_bitcast_fusion) | data formatting | bytes 8388608 | tf_op jit(solution)/shard_map/add | solution.py:108
  391.9 4.3 fusion.1
  396.3 16.9 %fusion = bf16[4096,256]{0,1:T(8,128)(2,1)} fusion(bf16[256,4096]{1,0:T(8,128)(2,1)} %fusion.1, bf16[4096,4096]{1,0:T(8,128)(2,1)} %all-gather.7.cloned.1.call-done), kind=kOutput, calls=%fused_computation.4 | convolution fusion | flops 8590983168 | bytes 37748736 | tf_op jit(solution)/shard_map/dot_general | solution.py:110
  413.2 48.4 %reduce-scatter.2.cloned.1.call-done = bf16[2048,256]{0,1:T(8,128)(2,1)} async-done(((bf16[4096,256]{0,1:T(8,128)(2,1)}), bf16[2048,256]{0,1:T(8,128)(2,1)}) %reduce-scatter.2.cloned.1.call-update) | async-done | bytes 1048592 | tf_op jit(solution)/shard_map/reduce_scatter | solution.py:116
  461.6 2.3 copy.92
  (63 shorter events, 2.8 us)
Async XLA Ops:
  6.5 166.3 %all-gather.9.cloned.1.call-start = ((), (), s32[]{:S(2)}) async-start(), calls=%async_computation.4 | async-start | bytes 4456448 | tf_op jit(solution)/shard_map/all_gather | solution.py:16
  7.4 32.7 %collective-permute-start.1 = (bf16[2,4096]{1,0:T(2,128)(2,1)S(1)}, bf16[2,4096]{1,0:T(2,128)(2,1)S(1)}, u32[]{:S(2)}, u32[]{:S(2)}) collective-permute-start(bf16[2,4096]{1,0:T(2,128)(2,1)S(1)} %slice.217), channel_id=1, source_target_pairs={{0,1},{1,2},{2,3},{3,4},{4,5},{5,6},{6,7},{7,8},{8,9},{9,10},{10,1... | collective-permute-start | bytes 49160 | tf_op jit(solution)/shard_map/ppermute | solution.py:11
  10.6 29.5 %collective-permute-start.2 = (bf16[2,4096]{1,0:T(2,128)(2,1)S(1)}, bf16[2,4096]{1,0:T(2,128)(2,1)S(1)}, u32[]{:S(2)}, u32[]{:S(2)}) collective-permute-start(bf16[2,4096]{1,0:T(2,128)(2,1)S(1)} %slice.227), channel_id=1, source_target_pairs={{0,1},{1,2},{2,3},{3,4},{4,5},{5,6},{6,7},{7,8},{8,9},{9,10},{10,1... | collective-permute-start | bytes 49160 | tf_op jit(solution)/shard_map/ppermute | solution.py:11
  17.2 22.9 %copy-start.2 = (f32[16,4096]{1,0:T(8,128)}, f32[16,4096]{1,0:T(8,128)S(1)}, u32[]{:S(2)}) copy-start(f32[16,4096]{1,0:T(8,128)S(1)} %get-tuple-element.82) | copy-start | bytes 786436
  17.2 99.4 %copy-start.6 = (f32[16,4096]{1,0:T(8,128)}, f32[16,4096]{1,0:T(8,128)S(1)}, u32[]{:S(2)}) copy-start(f32[16,4096]{1,0:T(8,128)S(1)} %get-tuple-element.80) | copy-start | bytes 786436
  17.2 102.6 %copy-start.4 = (f32[16,4096]{1,0:T(8,128)}, f32[16,4096]{1,0:T(8,128)S(1)}, u32[]{:S(2)}) copy-start(f32[16,4096]{1,0:T(8,128)S(1)} %get-tuple-element.78) | copy-start | bytes 786436
  17.2 182.5 %all-gather.5.cloned.1.call-start = ((), (), s32[]{:S(2)}) async-start(), calls=%async_computation.1 | async-start | bytes 4456448 | tf_op jit(solution)/shard_map/all_gather | solution.py:16
  119.1 1.0 copy-start.1
  120.2 0.7 copy-start
  124.7 9.8 %copy-start.5 = (f32[16,4096]{1,0:T(8,128)S(1)}, f32[16,4096]{1,0:T(8,128)}, u32[]{:S(2)}) copy-start(f32[16,4096]{1,0:T(8,128)} %copy-done.4) | copy-start | bytes 786436
  148.6 247.7 %all-gather.7.cloned.1.call-start = ((), (), s32[]{:S(2)}) async-start(), calls=%async_computation.2 | async-start | bytes 35651584 | tf_op jit(solution)/shard_map/all_gather | solution.py:111
  149.3 9.6 %copy-start.7 = (f32[16,4096]{1,0:T(8,128)S(1)}, f32[16,4096]{1,0:T(8,128)}, u32[]{:S(2)}) copy-start(f32[16,4096]{1,0:T(8,128)} %copy-done.6) | copy-start | bytes 786436
  149.3 312.3 %reduce-scatter.2.cloned.1.call-start = ((), (), s32[]{:S(2)}) async-start(), calls=%async_computation.3 | async-start | bytes 3145728 | tf_op jit(solution)/shard_map/reduce_scatter | solution.py:116
  150.3 241.7 %collective-permute-start = (bf16[2,4096]{1,0:T(2,128)(2,1)S(1)}, bf16[2,4096]{1,0:T(2,128)(2,1)S(1)}, u32[]{:S(2)}, u32[]{:S(2)}) collective-permute-start(bf16[2,4096]{1,0:T(2,128)(2,1)S(1)} %slice.207), channel_id=1, source_target_pairs={{0,1},{1,2},{2,3},{3,4},{4,5},{5,6},{6,7},{7,8},{8,9},{9,10},{10,1... | collective-permute-start | bytes 49160 | tf_op jit(solution)/shard_map/ppermute | solution.py:11
  172.8 27.2 %copy-start.3 = (f32[16,4096]{1,0:T(8,128)S(1)}, f32[16,4096]{1,0:T(8,128)}, u32[]{:S(2)}) copy-start(f32[16,4096]{1,0:T(8,128)} %copy-done.2) | copy-start | bytes 786436
  172.8 27.2 %copy-start.9 = (f32[16,4096]{1,0:T(8,128)S(1)}, f32[16,4096]{1,0:T(8,128)}, u32[]{:S(2)}) copy-start(f32[16,4096]{1,0:T(8,128)} %get-tuple-element.77) | copy-start | bytes 786436
  223.9 17.9 %copy-start.10 = (f32[16,16,16]{2,1,0:T(8,128)S(1)}, f32[16,16,16]{2,1,0:T(8,128)}, u32[]{:S(2)}) copy-start(f32[16,16,16]{2,1,0:T(8,128)} %constant.42.clone) | copy-start | bytes 49156
  372.0 19.9 %copy-start.8 = (bf16[256,4096]{1,0:T(8,128)(2,1)S(1)}, bf16[256,4096]{1,0:T(8,128)(2,1)}, u32[]{:S(2)}) copy-start(bf16[256,4096]{1,0:T(8,128)(2,1)} %param.10) | copy-start | bytes 6291460
Sparse Core Ops, SparseCore 0:
  17.4 50.8 all-gather.8
  148.7 50.9 all-gather.4
  201.3 166.5 all-gather.6
  413.3 48.2 reduce-scatter.1
where the time goes:
time: 473 us; the launch traced here: 470 us
  matrix products  165 us (35%)
  local copies, waits for them, and re-layouts  163 us (34%)
  waiting for transfers between devices  76.1 us (16%)
  other arithmetic  44 us (9%)
  between operations  13.4 us (3%)
  starting transfers between devices  9.05 us (2%)
    dot_general x1, matrix products, per_device(): jnp.einsum('qmc,smc->qsc', prior * mode_scale[None], lead_powers, precisi...  61 us
    reduce_scatter x1, waiting for transfers between devices, per_device(): lax.psum_scatter(partial_terms.astype(jnp.bfloat16), 'tensor', scatter_di...  48.4 us
    dot_general x1, matrix products, per_device(): jnp.einsum('qsc,stc->qtc', local_rows, toeplitz, precision=lax.Precision....  46.3 us
    dot_general x1, matrix products, per_device(): jnp.einsum('qsc,smc->qmc', local_rows, tail_powers, precision=lax.Precisi...  35.8 us
    all_gather x2, waiting for transfers between devices, prefix(): gathered = jax.tree.map(lambda a: lax.all_gather(a, axis), part)  26.9 us
    pad x6, local copies, waits for them, and re-layouts, per_device(): ignored, carried = lax.associative_scan(compose, (step_decay, sub_ends))  21.4 us
    add x1, local copies, waits for them, and re-layouts, per_device(): modal_out = (local_part + carried_part).reshape(row_count, chan_count)  19.9 us
    dot_general x1, local copies, waits for them, and re-layouts, per_device(): jnp.einsum('qsc,smc->qmc', local_rows, tail_powers, precision=lax.Precisi...  19.8 us
  transfers between devices with their start and end apart: 7, of which 2 were waited for; matrix products, arithmetic and copies ran while one was open for 75% of the time, Pallas kernels for 0%

commit v1 on v0

v1 whole, which is shorter than its diff:
```python
import functools

import jax
import jax.numpy as jnp
from jax import lax
from jax.experimental import pallas as pl
from jax.experimental.pallas import tpu as pltpu
from jax.sharding import PartitionSpec as P

LANES = 128
SEGS = 8
CREW = 4
PLANES = 4
F32 = jnp.float32
BF16 = jnp.bfloat16


def lane_block(chan_count):
    return 512 if chan_count % 512 == 0 else LANES


def tree_sum(terms):
    terms = list(terms)
    while len(terms) > 1:
        paired = [terms[i] + terms[i + 1] for i in range(0, len(terms) - 1, 2)]
        if len(terms) % 2:
            paired.append(terms[-1])
        terms = paired
    return terms[0]


def spread(row):
    return jnp.broadcast_to(row, (SEGS, LANES))


def local_kernel(
    total, q_ref, k_ref, v_ref, rim_ref, taps_ref, decay_ref, residue_ref,
    qf_ref, y_ref, carry_ref, end_ref, shifted, signal,
):
    rows, width = q_ref.shape
    modes = decay_ref.shape[0]
    length = rows // SEGS
    tap_count = taps_ref.shape[0] // 3
    lead = tap_count - 1

    def short_pass(which, ref, lanes):
        pad = shifted.at[which]
        pad[SEGS : SEGS + rows, :] = ref[:, lanes].astype(F32)
        pad[SEGS - lead : SEGS, :] = rim_ref[which * lead : (which + 1) * lead, lanes]
        running = None
        for offset in range(tap_count):
            row = which * tap_count + offset
            term = taps_ref[row : row + 1, lanes] * pad[SEGS - offset : SEGS - offset + rows, :]
            running = term if running is None else running + term
        return running.astype(BF16)

    for block in range(width // LANES):
        lanes = slice(block * LANES, (block + 1) * LANES)
        qf_ref[:, lanes] = short_pass(0, q_ref, lanes)
        k_feat = short_pass(1, k_ref, lanes).astype(F32)
        v_feat = short_pass(2, v_ref, lanes).astype(F32)
        signal[block] = (k_feat * v_feat).astype(BF16).astype(F32)

    seg = lax.broadcasted_iota(jnp.int32, (SEGS, LANES), 0)
    for block in range(width // LANES):
        lanes = slice(block * LANES, (block + 1) * LANES)
        steps = decay_ref[:, lanes] / total
        decays = jnp.exp(-steps)
        scales = residue_ref[:, lanes] * jnp.sqrt(2.0 * steps)
        decay = [spread(decays[m : m + 1]) for m in range(modes)]
        scale = [spread(scales[m : m + 1]) for m in range(modes)]

        def advance(i, state):
            x = signal[block, pl.ds(i, SEGS, stride=length), :]
            state = tuple(d * s + x for d, s in zip(decay, state))
            y_ref[i, :, lanes] = tree_sum(c * s for c, s in zip(scale, state))
            return state

        zero = jnp.zeros((SEGS, LANES), F32)
        state = lax.fori_loop(0, length, advance, (zero,) * modes, unroll=4)
        for m in range(modes):
            ends = state[m]
            for hop in (1, 2, 4):
                factor = spread(jnp.exp(-steps[m : m + 1] * float(length * hop)))
                ends = ends + factor * jnp.where(seg >= hop, pltpu.roll(ends, hop, 0), 0.0)
            end_ref[m : m + 1, lanes] = ends[SEGS - 1 : SEGS]
            carry_ref[m, :, lanes] = jnp.where(seg >= 1, pltpu.roll(ends, 1, 0), 0.0)


def gate_kernel(
    total, qf_ref, y_ref, carry_ref, incoming_ref, decay_ref, residue_ref, out_ref, mixed
):
    rows, width = qf_ref.shape
    modes = decay_ref.shape[0]
    length = rows // SEGS
    begin = (lax.broadcasted_iota(jnp.int32, (SEGS, LANES), 0) * length).astype(F32)
    for block in range(width // LANES):
        lanes = slice(block * LANES, (block + 1) * LANES)
        steps = decay_ref[:, lanes] / total
        decays = jnp.exp(-steps)
        weights = residue_ref[:, lanes] * jnp.sqrt(2.0 * steps) * decays
        decay = [spread(decays[m : m + 1]) for m in range(modes)]
        tail = []
        for m in range(modes):
            reach = jnp.exp(-spread(steps[m : m + 1]) * begin)
            held = carry_ref[m, :, lanes] + reach * spread(incoming_ref[m : m + 1, lanes])
            tail.append(spread(weights[m : m + 1]) * held)

        def advance(i, tail):
            mixed[block, pl.ds(i, SEGS, stride=length), :] = y_ref[i, :, lanes] + tree_sum(tail)
            return tuple(d * s for d, s in zip(decay, tail))

        lax.fori_loop(0, length, advance, tuple(tail), unroll=4)
    for block in range(width // LANES):
        lanes = slice(block * LANES, (block + 1) * LANES)
        out_ref[:, lanes] = (qf_ref[:, lanes].astype(F32) * mixed[block]).astype(BF16)


def local_pass(q_proj, k_proj, v_proj, rims, taps, decay_rate, residue, total):
    rows, chan_count = q_proj.shape
    modes = decay_rate.shape[0]
    width = lane_block(chan_count)
    length = rows // SEGS

    def cols(height):
        return pl.BlockSpec((height, width), lambda c: (0, c))

    return pl.pallas_call(
        functools.partial(local_kernel, total),
        grid=(chan_count // width,),
        in_specs=[
            cols(rows), cols(rows), cols(rows), cols(rims.shape[0]), cols(taps.shape[0]),
            cols(modes), cols(modes),
        ],
        out_specs=[
            cols(rows),
            pl.BlockSpec((length, SEGS, width), lambda c: (0, 0, c)),
            pl.BlockSpec((modes, SEGS, width), lambda c: (0, 0, c)),
            cols(modes),
        ],
        out_shape=[
            jax.ShapeDtypeStruct((rows, chan_count), BF16),
            jax.ShapeDtypeStruct((length, SEGS, chan_count), F32),
            jax.ShapeDtypeStruct((modes, SEGS, chan_count), F32),
            jax.ShapeDtypeStruct((modes, chan_count), F32),
        ],
        scratch_shapes=[
            pltpu.VMEM((3, rows + SEGS, LANES), F32),
            pltpu.VMEM((width // LANES, rows, LANES), F32),
        ],
        compiler_params=pltpu.CompilerParams(vmem_limit_bytes=32 * 2**20),
        name="local_pass",
    )(q_proj, k_proj, v_proj, rims, taps, decay_rate, residue)


def gate_pass(q_feat, y_local, carry, incoming, decay_rate, residue, total):
    rows, chan_count = q_feat.shape
    modes = decay_rate.shape[0]
    width = lane_block(chan_count)
    length = rows // SEGS

    def cols(height):
        return pl.BlockSpec((height, width), lambda c: (0, c))

    return pl.pallas_call(
        functools.partial(gate_kernel, total),
        grid=(chan_count // width,),
        in_specs=[
            cols(rows),
            pl.BlockSpec((length, SEGS, width), lambda c: (0, 0, c)),
            pl.BlockSpec((modes, SEGS, width), lambda c: (0, 0, c)),
            cols(modes), cols(modes), cols(modes),
        ],
        out_specs=cols(rows),
        out_shape=jax.ShapeDtypeStruct((rows, chan_count), BF16),
        scratch_shapes=[pltpu.VMEM((width // LANES, rows, LANES), F32)],
        compiler_params=pltpu.CompilerParams(vmem_limit_bytes=32 * 2**20),
        name="gate_pass",
    )(q_feat, y_local, carry, incoming, decay_rate, residue)


def product_kernel(slot_count, pick_ref, *refs):
    pairs = [refs[2 * s : 2 * s + 2] for s in range(slot_count)]
    tokens = refs[2 * slot_count : 2 * slot_count + CREW]
    out_ref, total = refs[2 * slot_count + CREW :]
    feat = pairs[0][0].shape[0]
    step = pl.program_id(0)

    @pl.when(step == 0)
    def _():
        total[...] = jnp.zeros_like(total)

    for s, (one, other) in enumerate(pairs):
        for first, source in ((1, one), (0, other)):

            @pl.when(pick_ref[s] == first)
            def _():
                weights = source[...]
                for j in range(CREW):
                    total[j, s * feat : (s + 1) * feat, :] += lax.dot_general(
                        weights, tokens[j][...], (((1,), (1,)), ((), ())),
                        preferred_element_type=F32,
                    )

    @pl.when(step == pl.num_programs(0) - 1)
    def _():
        out_ref[...] = total[...].astype(BF16)


def project(pairs, picks, tokens):
    feat, depth = pairs[0][0].shape
    rows = tokens[0].shape[0]
    slot_count = len(pairs)
    width = 1024 if depth % 1024 == 0 else LANES
    flat = [array for pair in pairs for array in pair]
    out_rows = slot_count * feat
    return pl.pallas_call(
        functools.partial(product_kernel, slot_count),
        grid_spec=pltpu.PrefetchScalarGridSpec(
            num_scalar_prefetch=1,
            grid=(depth // width,),
            in_specs=[pl.BlockSpec((feat, width), lambda c, _: (0, c)) for _ in flat]
            + [pl.BlockSpec((rows, width), lambda c, _: (0, c)) for _ in tokens],
            out_specs=pl.BlockSpec((CREW, out_rows, rows), lambda c, _: (0, 0, 0)),
            scratch_shapes=[pltpu.VMEM((CREW, out_rows, rows), F32)],
        ),
        out_shape=jax.ShapeDtypeStruct((CREW, out_rows, rows), BF16),
        compiler_params=pltpu.CompilerParams(vmem_limit_bytes=48 * 2**20),
        name="project",
    )(jnp.stack(picks).astype(jnp.int32), *flat, *tokens)


def assemble_kernel(place_ref, *refs):
    near, third, fourth, out_ref = refs[:CREW], refs[CREW : 2 * CREW], refs[2 * CREW : -1], refs[-1]
    feat = third[0].shape[0]
    half = out_ref.shape[0] // 2
    same, low, seat = place_ref[0], place_ref[1], place_ref[2]
    for j in range(CREW):
        within = (seat ^ j) * feat
        first = pl.multiple_of(low * half + within, feat)
        second = pl.multiple_of((1 - low) * half + within, feat)

        @pl.when(same == 1)
        def _():
            out_ref[pl.ds(first, feat), :] = near[j][:feat, :]
            out_ref[pl.ds(second, feat), :] = near[j][feat:, :]

        @pl.when(same == 0)
        def _():
            out_ref[pl.ds(first, feat), :] = third[j][...]
            out_ref[pl.ds(second, feat), :] = fourth[j][...]


def assemble(place, near, third, fourth):
    feat, rows = third[0].shape
    vmem = pl.BlockSpec(memory_space=pltpu.VMEM)
    return pl.pallas_call(
        assemble_kernel,
        in_specs=[pl.BlockSpec(memory_space=pltpu.SMEM)] + [vmem] * (3 * CREW),
        out_specs=vmem,
        out_shape=jax.ShapeDtypeStruct((2 * CREW * feat, rows), BF16),
        name="assemble",
    )(place, *near, *third, *fourth)


def widen_taps(short_filter, chan_count):
    kinds, tap_count, groups = short_filter.shape
    return jnp.repeat(
        short_filter.astype(F32).reshape(kinds * tap_count, groups), chan_count // groups, axis=1
    )


def gather_rims(q_proj, k_proj, v_proj, lead):
    size = lax.axis_size("context")
    tails = jnp.concatenate([a[a.shape[0] - lead :] for a in (q_proj, k_proj, v_proj)], axis=0)
    rims = lax.ppermute(tails, "context", [(i, i + 1) for i in range(size - 1)])
    return jnp.pad(rims.astype(F32), ((0, -rims.shape[0] % SEGS), (0, 0)))


def per_device(q_proj, k_proj, v_proj, short_filter, residue, decay_rate, out_weight):
    rows, chan_count = q_proj.shape
    size = lax.axis_size("context")
    total = float(rows * size)
    place = lax.axis_index("context")
    rims = gather_rims(q_proj, k_proj, v_proj, short_filter.shape[1] - 1)
    taps = widen_taps(short_filter, chan_count)
    q_feat, y_local, carry, ends = local_pass(
        q_proj, k_proj, v_proj, rims, taps, decay_rate, residue, total
    )
    gathered = lax.all_gather(ends, "context")
    gaps = (place - 1 - jnp.arange(size))[:, None, None]
    reach = jnp.exp(-(decay_rate / total)[None] * (gaps * rows).astype(F32))
    incoming = jnp.sum(jnp.where(gaps >= 0, reach * gathered, 0.0), axis=0)
    gated = gate_pass(q_feat, y_local, carry, incoming, decay_rate, residue, total)
    partial_terms = lax.dot_general(
        lax.all_gather(out_weight, "context", axis=0, tiled=True),
        gated,
        (((1,), (1,)), ((), ())),
        preferred_element_type=F32,
    )
    return lax.psum_scatter(
        partial_terms.astype(BF16), "tensor", scatter_dimension=0, tiled=True
    )


def swap(block, mask):
    size = lax.axis_size("context")
    return lax.ppermute(block, "context", [(i, i ^ mask) for i in range(size)])


def shift(block, distance):
    size = lax.axis_size("context")
    moves = [(i, i + distance) for i in range(size) if 0 <= i + distance < size]
    return lax.ppermute(block, "context", moves)


def exchange_states(ends, steps, rows, place):
    chan_count = ends.shape[1]
    quarter = chan_count // CREW
    seat = place % CREW

    def part(array, owner):
        return lax.dynamic_slice_in_dim(array, owner * quarter, quarter, 1)

    own_steps = part(steps, seat)

    def reach(count):
        return jnp.exp(-own_steps * (rows * count).astype(F32))

    blocks = [part(ends, seat)] + [swap(part(ends, seat ^ j), j) for j in range(1, CREW)]
    plane = sum(reach(CREW - 1 - (seat ^ j)) * blocks[j] for j in range(CREW))
    before = jnp.zeros_like(plane)
    for hop in range(1, PLANES):
        arrived = shift(plane, hop * CREW)
        before = before + jnp.exp(-own_steps * float(rows * CREW * (hop - 1))) * arrived

    def for_seat(target):
        state = reach(target) * before
        for j in range(CREW):
            gap = target - 1 - (seat ^ j)
            state = state + jnp.where(gap >= 0, reach(jnp.maximum(gap, 0)) * blocks[j], 0.0)
        return state

    mine = [for_seat(seat)] + [swap(for_seat(seat ^ j), j) for j in range(1, CREW)]
    odd, high = seat % 2 == 1, seat >= 2
    ordered = [jnp.where(odd, mine[j ^ 1], mine[j]) for j in range(CREW)]
    ordered = [jnp.where(high, ordered[j ^ 2], ordered[j]) for j in range(CREW)]
    return jnp.concatenate(ordered, axis=1)


def per_device_planes(q_proj, k_proj, v_proj, short_filter, residue, decay_rate, out_weight):
    rows, chan_count = q_proj.shape
    size = lax.axis_size("context")
    total = float(rows * size)
    place = lax.axis_index("context")
    side = lax.axis_index("tensor")
    plane, seat = place // CREW, place % CREW
    low = plane % 2
    same = (side == plane // 2).astype(jnp.int32)

    up1, down1 = shift(out_weight, CREW), shift(out_weight, -CREW)
    rims = gather_rims(q_proj, k_proj, v_proj, short_filter.shape[1] - 1)
    taps = widen_taps(short_filter, chan_count)
    q_feat, y_local, carry, ends = local_pass(
        q_proj, k_proj, v_proj, rims, taps, decay_rate, residue, total
    )
    incoming = exchange_states(ends, decay_rate / total, rows, place)
    gated = gate_pass(q_feat, y_local, carry, incoming, decay_rate, residue, total)

    def hops(block, moves):
        return lax.ppermute(
            block, "context",
            [(a * CREW + s, b * CREW + s) for a, b in moves for s in range(CREW)],
        )

    up2 = hops(up1, [(1, 2), (2, 3)])
    down2 = hops(down1, [(2, 1), (1, 0)])
    up3 = hops(up2, [(2, 3)])
    down3 = hops(down2, [(1, 0)])

    tokens = [gated, swap(gated, 1), swap(gated, 2)]
    tokens.append(swap(tokens[2], 1))

    def cross(block, from_same):
        moves = []
        for p in range(PLANES):
            for s in range(CREW):
                keeper = p // 2 if not from_same else 1 - p // 2
                moves.append(((1 - keeper) * size + p * CREW + s, keeper * size + p * CREW + s))
        return lax.ppermute(block, ("tensor", "context"), moves)

    def deal(block, mask, to_same):
        moves = []
        for p in range(PLANES):
            keeper = p // 2 if to_same else 1 - p // 2
            for s in range(CREW):
                at = keeper * size + p * CREW
                moves.append((at + s, at + (s ^ mask)))
        return lax.ppermute(block, ("tensor", "context"), moves)

    def finish(partials, to_same):
        arrived = cross(partials, not to_same)
        summed = [
            (partials[j].astype(F32) + arrived[j].astype(F32)).astype(BF16) for j in range(CREW)
        ]
        return [summed[0]] + [deal(summed[j], j, to_same) for j in range(1, CREW)]

    edge = (plane == 0) | (plane == PLANES - 1)
    near = project([(out_weight, out_weight), (up1, down1)], [low * 0 + 1, low], tokens)
    near = finish(near, True)
    third = project([(up2, down2)], [plane >= 2], tokens)
    third = finish(third, False)
    middle = jnp.where(plane == 1, down1, up1)
    outer = jnp.where(plane == 0, down3, up3)
    fourth = project([(outer, middle)], [edge], tokens)
    fourth = finish(fourth, False)
    return assemble(jnp.stack([same, low, seat]).astype(jnp.int32), near, third, fourth)


def solution(mesh):
    planes = mesh.shape["tensor"] == 2 and mesh.shape["context"] == CREW * PLANES
    return jax.shard_map(
        per_device_planes if planes else per_device,
        mesh=mesh,
        in_specs=(
            P("context", "tensor"),
            P("context", "tensor"),
            P("context", "tensor"),
            P(None, None, "tensor"),
            P(None, "tensor"),
            P(None, "tensor"),
            P("context", "tensor"),
        ),
        out_specs=P("tensor", "context"),
        check_vma=False,
    )
```

time: 473 us -> 223 us (0.47)
  matrix products: 165 us -> 0 us
  local copies, waits for them, and re-layouts: 163 us -> 21.1 us
  Pallas kernels: 0 us -> 52 us
  starting transfers between devices: 9.05 us -> 52.2 us
  other arithmetic: 44 us -> 7.49 us
  between operations: 13.4 us -> 0.69 us
  waiting for transfers between devices: 76.1 us -> 85 us
    dot_general x5 -> x0, matrix products: 165 us -> none  [the longest x1 61 us: per_device(): jnp.einsum('qmc,smc->qsc', prior * mode_scale[None], lead_powers, precisi...]
    ppermute x3 -> x31, waiting for transfers between devices: 0.01 us -> 85 us  [the longest x9 50.5 us: swap(): return lax.ppermute(block, 'context', [(i, i ^ mask) for i in range(size)])]
    pallas_call x0 -> x6, Pallas kernels: none -> 52 us  [the longest x3 21.7 us: project(): pl.pallas_call(functools.partial(product_kernel, slot_count), grid_spec=p...]
    reduce_scatter x1 -> x0, waiting for transfers between devices: 48.4 us -> none  [per_device(): lax.psum_scatter(partial_terms.astype(jnp.bfloat16), 'tensor', scatter_di...]
    ppermute x3 -> x31, starting transfers between devices: 8.93 us -> 52.2 us  [the longest x5 16.8 us: shift(): return lax.ppermute(block, 'context', moves)]
    dot_general x2 -> x0, local copies, waits for them, and re-layouts: 37.8 us -> none  [the longest x1 19.8 us: per_device(): jnp.einsum('qsc,smc->qmc', local_rows, tail_powers, precision=lax.Precisi...]
    exp x2 -> x0, local copies, waits for them, and re-layouts: 36.1 us -> none  [the longest x1 18.1 us: per_device(): lead_powers = jnp.exp(-decay_step[None] * (offsets + 1.0)[:, None, None])]
    all_gather x3 -> x0, waiting for transfers between devices: 26.9 us -> none  [the longest x2 26.9 us: prefix(): gathered = jax.tree.map(lambda a: lax.all_gather(a, axis), part)]
  transfers between devices with their start and end apart: 7 -> 31, of which waited for: 2 -> 11; matrix products, arithmetic and copies ran while one was open for 75% -> 5% of each run, Pallas kernels for 0% -> 23%
where the time goes in v1:
time: 223 us; the launch traced here: 219 us
  waiting for transfers between devices  85 us (38%)
  starting transfers between devices  52.2 us (23%)
  Pallas kernels  52 us (23%)
  local copies, waits for them, and re-layouts  21.1 us (9%)
  other arithmetic  7.49 us (3%)
    ppermute x9, waiting for transfers between devices, swap(): return lax.ppermute(block, 'context', [(i, i ^ mask) for i in range(size)])  50.5 us
    ppermute x4, waiting for transfers between devices, hops(): lax.ppermute(block, 'context', [(a * CREW + s, b * CREW + s) for a, b in...  25.1 us
    pallas_call x3, Pallas kernels, project(): pl.pallas_call(functools.partial(product_kernel, slot_count), grid_spec=p...  21.7 us
    pallas_call x1, Pallas kernels, local_pass(): pl.pallas_call(functools.partial(local_kernel, total), grid=(chan_count /...  19.7 us
    ppermute x5, starting transfers between devices, shift(): return lax.ppermute(block, 'context', moves)  16.8 us
    unnamed x44, local copies, waits for them, and re-layouts  14.3 us
    ppermute x9, starting transfers between devices, deal(): return lax.ppermute(block, ('tensor', 'context'), moves)  10.6 us
    ppermute x3, starting transfers between devices, cross(): return lax.ppermute(block, ('tensor', 'context'), moves)  9.36 us
  transfers between devices with their start and end apart: 31, of which 11 were waited for; matrix products, arithmetic and copies ran while one was open for 5% of the time, Pallas kernels for 23%

profile of v1, /device:TPU:0, one launch (start us, length us, event | category | flops | bytes accessed | tf_op | source)
XLA Modules:
  0.0 218.5 jit_solution(8808879777730078019)
XLA Ops:
  0.0 1.0 slice.83
  2.8 2.4 %collective-permute-start.2 = (bf16[6,4096]{1,0:T(8,128)(2,1)S(1)}, bf16[6,4096]{1,0:T(8,128)(2,1)S(1)}, u32[]{:S(2)}, u32[]{:S(2)}) collective-permute-start(bf16[6,4096]{1,0:T(8,128)(2,1)S(1)} %pad_maximum_fusion.1), channel_id=1, source_target_pairs={{0,1},{1,2},{2,3},{3,4},{4,5},{5,6},{6,7},{7,8},{8,9},{9,10},{10,1... | collective-permute-start | bytes 147464 | tf_op jit(solution)/shard_map/ppermute | solution.py:276
  5.2 5.9 %collective-permute-start = (bf16[256,4096]{1,0:T(8,128)(2,1)}, bf16[256,4096]{1,0:T(8,128)(2,1)}, u32[]{:S(2)}, u32[]{:S(2)}) collective-permute-start(bf16[256,4096]{1,0:T(8,128)(2,1)} %refs_1_.1), channel_id=1, source_target_pairs={{0,4},{1,5},{2,6},{3,7},{4,8},{5,9},{6,10},{7,11},{8,12},{9,13},{1... | collective-permute-start | bytes 6291464 | tf_op jit(solution)/shard_map/ppermute | solution.py:314
  11.1 1.3 collective-permute-start.1
  13.1 1.4 broadcast_in_dim.20
  14.5 2.0 reshape.63.taps_ref
  16.6 1.6 copy-done.6
  18.1 1.6 copy-done.7
  19.7 19.7 %local_pass.1 = (bf16[256,4096]{1,0:T(8,128)(2,1)S(1)}, f32[32,8,4096]{2,1,0:T(8,128)S(1)}, f32[16,8,4096]{2,1,0:T(8,128)S(1)}, f32[16,4096]{1,0:T(8,128)S(1)}) custom-call(bf16[256,4096]{1,0:T(8,128)(2,1)S(1)} %copy-done.5, bf16[256,4096]{1,0:T(8,128)(2,1)S(1)} %copy-done.6, bf16[256,4096]{1,0:T(8,128)(2,1)S(1)} %copy-done.7, ...), custom_call_target="tpu_custom_call" | custom-call | tf_op jit(solution)/shard_map/local_pass/pallas_call | solution.py:128
  39.5 2.0 copy-done.2
  41.4 1.3 copy-done.8
  42.8 1.4 copy-done.10
  44.2 2.5 %collective-permute-start.5 = (f32[16,1024]{1,0:T(8,128)S(1)}, f32[16,1024]{1,0:T(8,128)S(1)}, u32[]{:S(2)}, u32[]{:S(2)}) collective-permute-start(f32[16,1024]{1,0:T(8,128)S(1)} %get-tuple-element.33), channel_id=1, source_target_pairs={{0,3},{1,2},{2,1},{3,0},{4,7},{5,6},{6,5},{7,4},{8,11},{9,10},{10,... | collective-permute-start | bytes 196616 | tf_op jit(solution)/shard_map/ppermute | solution.py:308
  47.2 1.9 collective-permute-done.5
  49.2 2.1 collective-permute-done.4
  51.3 5.9 %collective-permute-start.8 = (f32[16,1024]{1,0:T(8,128)S(1)}, f32[16,1024]{1,0:T(8,128)S(1)}, u32[]{:S(2)}, u32[]{:S(2)}) collective-permute-start(f32[16,1024]{1,0:T(8,128)S(1)} %multiply_add_fusion.1), channel_id=1, source_target_pairs={{0,12},{1,13},{2,14},{3,15},{16,28},{17,29},{18,30},{19,31}} | collective-permute-start | bytes 196616 | tf_op jit(solution)/shard_map/ppermute | solution.py:314
  57.2 1.3 collective-permute-start.7
  58.5 2.5 %collective-permute-start.6 = (f32[16,1024]{1,0:T(8,128)S(1)}, f32[16,1024]{1,0:T(8,128)S(1)}, u32[]{:S(2)}, u32[]{:S(2)}) collective-permute-start(f32[16,1024]{1,0:T(8,128)S(1)} %multiply_add_fusion.1), channel_id=1, source_target_pairs={{0,4},{1,5},{2,6},{3,7},{4,8},{5,9},{6,10},{7,11},{8,12},{9,13},{1... | collective-permute-start | bytes 196616 | tf_op jit(solution)/shard_map/ppermute | solution.py:314
  61.1 1.8 collective-permute-done.6
  64.2 1.2 collective-permute-start.11
  65.4 2.3 %collective-permute-done.10 = f32[16,1024]{1,0:T(8,128)S(1)} collective-permute-done((f32[16,1024]{1,0:T(8,128)S(1)}, f32[16,1024]{1,0:T(8,128)S(1)}, u32[]{:S(2)}, u32[]{:S(2)}) %collective-permute-start.10) | collective-permute-done | bytes 65568 | tf_op jit(solution)/shard_map/ppermute | solution.py:308
  68.6 2.2 copy-done.3
  70.8 1.6 copy-done.9
  72.4 1.6 copy-done.11
  74.0 8.0 %gate_pass.1.refs_4_.refs_2_ = bf16[256,4096]{1,0:T(8,128)(2,1)S(1)} custom-call(bf16[256,4096]{1,0:T(8,128)(2,1)S(1)} %copy-done.9, f32[32,8,4096]{2,1,0:T(8,128)S(1)} %copy-done.3, f32[16,8,4096]{2,1,0:T(8,128)S(1)} %copy-done.11, f32[16,4096]{1,0:T(8,128)S(1)} %pad_maximum_fusion.incoming_ref, f32[16,4096]{1,0:T(8,128)S(1)} %copy-done.4, ...), custom_call_target="tpu_custom_call" | custom-call | tf_op jit(solution)/shard_map/gate_pass/pallas_call | solution.py:165
  82.0 1.2 collective-permute-start.13
  83.2 1.3 collective-permute-start.20
  84.5 2.0 collective-permute-start.19
  86.5 43.4 %collective-permute-done.13.refs_6_.refs_4_ = bf16[256,4096]{1,0:T(8,128)(2,1)} collective-permute-done((bf16[256,4096]{1,0:T(8,128)(2,1)S(1)}, bf16[256,4096]{1,0:T(8,128)(2,1)}, u32[]{:S(2)}, u32[]{:S(2)}) %collective-permute-start.13) | collective-permute-done | bytes 2097184 | tf_op jit(solution)/shard_map/ppermute | solution.py:308
  129.8 3.5 %collective-permute-done.20.refs_1_ = bf16[256,4096]{1,0:T(8,128)(2,1)} collective-permute-done((bf16[256,4096]{1,0:T(8,128)(2,1)}, bf16[256,4096]{1,0:T(8,128)(2,1)}, u32[]{:S(2)}, u32[]{:S(2)}) %collective-permute-start.20) | collective-permute-done | bytes 2097184 | tf_op jit(solution)/shard_map/ppermute | solution.py:371
  133.4 1.3 collective-permute-start.25
  134.7 2.0 collective-permute-start.26
  136.8 2.0 broadcast_select_fusion.refs_1_
  139.0 9.3 %project.3 = bf16[4,512,256]{2,1,0:T(8,128)(2,1)S(1)} custom-call(s32[2]{0:T(128)S(1)} %pad_add_fusion.1.pick_ref, bf16[256,4096]{1,0:T(8,128)(2,1)S(1)} %copy-done.1, bf16[256,4096]{1,0:T(8,128)(2,1)S(1)} %copy-done.1, bf16[256,4096]{1,0:T(8,128)(2,1)} %collective-permute-done.refs_2_, bf16[256,4096]{1,0:T(8,128)(2,1)} %collective-permute-done.1.refs_3_, ...), custom_call_target="tpu_custom_call" | custom-call | tf_op jit(solution)/shard_map/project/pallas_call | solution.py:217
  148.4 1.3 collective-permute-start.15
  149.7 6.5 %project.4 = bf16[4,256,256]{2,1,0:T(8,128)(2,1)S(1)} custom-call(s32[1]{0:T(128)} %bitcast.7.pick_ref, bf16[256,4096]{1,0:T(8,128)(2,1)} %collective-permute-done.19.refs_0_, bf16[256,4096]{1,0:T(8,128)(2,1)} %collective-permute-done.20.refs_1_, bf16[256,4096]{1,0:T(8,128)(2,1)} %copy-done, bf16[256,4096]{1,0:T(8,128)(2,1)} %collective-permute-done.12.refs_5_.refs_3_, ...), custom_call_target="tpu_custom_call" | custom-call | tf_op jit(solution)/shard_map/project/pallas_call | solution.py:217
  156.2 4.6 %collective-permute-start.21 = (bf16[4,256,256]{2,1,0:T(8,128)(2,1)S(1)}, bf16[4,256,256]{2,1,0:T(8,128)(2,1)S(1)}, u32[]{:S(2)}, u32[]{:S(2)}) collective-permute-start(bf16[4,256,256]{2,1,0:T(8,128)(2,1)S(1)} %project.4), channel_id=1, source_target_pairs={{0,16},{1,17},{2,18},{3,19},{4,20},{5,21},{6,22},{7,23},{24,8},{25... | collective-permute-start | bytes 1572872 | tf_op jit(solution)/shard_map/ppermute | solution.py:390
  160.8 21.6 %collective-permute-done.25 = bf16[256,4096]{1,0:T(8,128)(2,1)} collective-permute-done((bf16[256,4096]{1,0:T(8,128)(2,1)}, bf16[256,4096]{1,0:T(8,128)(2,1)}, u32[]{:S(2)}, u32[]{:S(2)}) %collective-permute-start.25) | collective-permute-done | bytes 2097184 | tf_op jit(solution)/shard_map/ppermute | solution.py:371
  182.4 1.8 broadcast_select_fusion.1.refs_0_
  184.2 5.9 %project.5 = bf16[4,256,256]{2,1,0:T(8,128)(2,1)S(1)} custom-call(s32[1]{0:T(128)} %bitcast.12.pick_ref, bf16[256,4096]{1,0:T(8,128)(2,1)S(1)} %broadcast_select_fusion.1.refs_0_, bf16[256,4096]{1,0:T(8,128)(2,1)S(1)} %broadcast_select_fusion.refs_1_, bf16[256,4096]{1,0:T(8,128)(2,1)} %copy-done, bf16[256,4096]{1,0:T(8,128)(2,1)} %collective-permute-done.12.refs_5_.refs_3_, ...), custom_call_target="tpu_custom_call" | custom-call | tf_op jit(solution)/shard_map/project/pallas_call | solution.py:217
  190.1 3.4 %collective-permute-start.27 = (bf16[4,256,256]{2,1,0:T(8,128)(2,1)S(1)}, bf16[4,256,256]{2,1,0:T(8,128)(2,1)S(1)}, u32[]{:S(2)}, u32[]{:S(2)}) collective-permute-start(bf16[4,256,256]{2,1,0:T(8,128)(2,1)S(1)} %project.5), channel_id=1, source_target_pairs={{0,16},{1,17},{2,18},{3,19},{4,20},{5,21},{6,22},{7,23},{24,8},{25... | collective-permute-start | bytes 1572872 | tf_op jit(solution)/shard_map/ppermute | solution.py:390
  196.0 1.9 collective-permute-start.16
  199.3 2.8 %collective-permute-start.17 = (bf16[512,256]{1,0:T(8,128)(2,1)S(1)}, bf16[512,256]{1,0:T(8,128)(2,1)S(1)}, u32[]{:S(2)}, u32[]{:S(2)}) collective-permute-start(bf16[512,256]{1,0:T(8,128)(2,1)S(1)} %get-tuple-element.18), channel_id=1, source_target_pairs={{0,2},{1,3},{2,0},{3,1},{4,6},{5,7},{6,4},{7,5},{24,26},{25,27},{2... | collective-permute-start | bytes 786440 | tf_op jit(solution)/shard_map/ppermute | solution.py:399
  202.1 1.1 collective-permute-done.27
  203.2 1.9 collective-permute-start.18
  208.7 1.6 collective-permute-done.17.refs_2_
  210.3 4.8 %collective-permute-done.18.refs_3_ = bf16[512,256]{1,0:T(8,128)(2,1)S(1)} collective-permute-done((bf16[512,256]{1,0:T(8,128)(2,1)S(1)}, bf16[512,256]{1,0:T(8,128)(2,1)S(1)}, u32[]{:S(2)}, u32[]{:S(2)}) %collective-permute-start.18) | collective-permute-done | bytes 262176 | tf_op jit(solution)/shard_map/ppermute | solution.py:399
  216.0 2.6 %assemble.1 = bf16[2048,256]{1,0:T(8,128)(2,1)} custom-call(s32[3]{0:T(128)} %pad_add_fusion.place_ref, bf16[512,256]{1,0:T(8,128)(2,1)} %get-tuple-element.20.refs_0_, bf16[512,256]{1,0:T(8,128)(2,1)} %copy-done.13, bf16[512,256]{1,0:T(8,128)(2,1)} %copy-done.14, bf16[512,256]{1,0:T(8,128)(2,1)} %copy-done.15, bf16[256,256]{1,0:T(8,128)(2,1)} %get-tuple-element.28.refs_4_, ...), custom_call_target="tpu_custom_call" | custom-call | tf_op jit(solution)/shard_map/assemble/pallas_call | solution.py:257
  (87 shorter events, 13.7 us)
Async XLA Ops:
  0.0 16.5 %copy-start.5 = (bf16[256,4096]{1,0:T(8,128)(2,1)S(1)}, bf16[256,4096]{1,0:T(8,128)(2,1)}, u32[]{:S(2)}) copy-start(bf16[256,4096]{1,0:T(8,128)(2,1)} %q_ref.1) | copy-start | bytes 6291460
  0.0 16.5 %copy-start.4 = (f32[16,4096]{1,0:T(8,128)S(1)}, f32[16,4096]{1,0:T(8,128)}, u32[]{:S(2)}) copy-start(f32[16,4096]{1,0:T(8,128)} %decay_ref.3) | copy-start | bytes 786436
  0.0 16.5 %copy-start.12 = (f32[16,4096]{1,0:T(8,128)S(1)}, f32[16,4096]{1,0:T(8,128)}, u32[]{:S(2)}) copy-start(f32[16,4096]{1,0:T(8,128)} %residue_ref.3) | copy-start | bytes 786436
  2.8 13.7 %collective-permute-start.2 = (bf16[6,4096]{1,0:T(8,128)(2,1)S(1)}, bf16[6,4096]{1,0:T(8,128)(2,1)S(1)}, u32[]{:S(2)}, u32[]{:S(2)}) collective-permute-start(bf16[6,4096]{1,0:T(8,128)(2,1)S(1)} %pad_maximum_fusion.1), channel_id=1, source_target_pairs={{0,1},{1,2},{2,3},{3,4},{4,5},{5,6},{6,7},{7,8},{8,9},{9,10},{10,1... | collective-permute-start | bytes 147464 | tf_op jit(solution)/shard_map/ppermute | solution.py:276
  5.2 79.3 %collective-permute-start = (bf16[256,4096]{1,0:T(8,128)(2,1)}, bf16[256,4096]{1,0:T(8,128)(2,1)}, u32[]{:S(2)}, u32[]{:S(2)}) collective-permute-start(bf16[256,4096]{1,0:T(8,128)(2,1)} %refs_1_.1), channel_id=1, source_target_pairs={{0,4},{1,5},{2,6},{3,7},{4,8},{5,9},{6,10},{7,11},{8,12},{9,13},{1... | collective-permute-start | bytes 6291464 | tf_op jit(solution)/shard_map/ppermute | solution.py:314
  11.1 72.1 %collective-permute-start.1 = (bf16[256,4096]{1,0:T(8,128)(2,1)}, bf16[256,4096]{1,0:T(8,128)(2,1)}, u32[]{:S(2)}, u32[]{:S(2)}) collective-permute-start(bf16[256,4096]{1,0:T(8,128)(2,1)} %refs_1_.1), channel_id=1, source_target_pairs={{4,0},{5,1},{6,2},{7,3},{8,4},{9,5},{10,6},{11,7},{12,8},{13,9},{1... | collective-permute-start | bytes 6291464 | tf_op jit(solution)/shard_map/ppermute | solution.py:314
  16.5 1.6 copy-start.6
  18.1 1.6 copy-start.7
  39.4 2.0 copy-start.2
  42.8 1.4 copy-start.10
  44.2 5.0 %collective-permute-start.5 = (f32[16,1024]{1,0:T(8,128)S(1)}, f32[16,1024]{1,0:T(8,128)S(1)}, u32[]{:S(2)}, u32[]{:S(2)}) collective-permute-start(f32[16,1024]{1,0:T(8,128)S(1)} %get-tuple-element.33), channel_id=1, source_target_pairs={{0,3},{1,2},{2,1},{3,0},{4,7},{5,6},{6,5},{7,4},{8,11},{9,10},{10,... | collective-permute-start | bytes 196616 | tf_op jit(solution)/shard_map/ppermute | solution.py:308
  46.7 2.4 %collective-permute-start.3 = (f32[16,1024]{1,0:T(8,128)S(1)}, f32[16,1024]{1,0:T(8,128)S(1)}, u32[]{:S(2)}, u32[]{:S(2)}) collective-permute-start(f32[16,1024]{1,0:T(8,128)S(1)} %get-tuple-element.34), channel_id=1, source_target_pairs={{0,1},{1,0},{2,3},{3,2},{4,5},{5,4},{6,7},{7,6},{8,9},{9,8},{10,11... | collective-permute-start | bytes 196616 | tf_op jit(solution)/shard_map/ppermute | solution.py:308
  46.7 4.5 %collective-permute-start.4 = (f32[16,1024]{1,0:T(8,128)S(1)}, f32[16,1024]{1,0:T(8,128)S(1)}, u32[]{:S(2)}, u32[]{:S(2)}) collective-permute-start(f32[16,1024]{1,0:T(8,128)S(1)} %get-tuple-element.32), channel_id=1, source_target_pairs={{0,2},{1,3},{2,0},{3,1},{4,6},{5,7},{6,4},{7,5},{8,10},{9,11},{10,... | collective-permute-start | bytes 196616 | tf_op jit(solution)/shard_map/ppermute | solution.py:308
  51.3 9.8 %collective-permute-start.8 = (f32[16,1024]{1,0:T(8,128)S(1)}, f32[16,1024]{1,0:T(8,128)S(1)}, u32[]{:S(2)}, u32[]{:S(2)}) collective-permute-start(f32[16,1024]{1,0:T(8,128)S(1)} %multiply_add_fusion.1), channel_id=1, source_target_pairs={{0,12},{1,13},{2,14},{3,15},{16,28},{17,29},{18,30},{19,31}} | collective-permute-start | bytes 196616 | tf_op jit(solution)/shard_map/ppermute | solution.py:314
  57.2 3.9 %collective-permute-start.7 = (f32[16,1024]{1,0:T(8,128)S(1)}, f32[16,1024]{1,0:T(8,128)S(1)}, u32[]{:S(2)}, u32[]{:S(2)}) collective-permute-start(f32[16,1024]{1,0:T(8,128)S(1)} %multiply_add_fusion.1), channel_id=1, source_target_pairs={{0,8},{1,9},{2,10},{3,11},{4,12},{5,13},{6,14},{7,15},{16,24},{17,... | collective-permute-start | bytes 196616 | tf_op jit(solution)/shard_map/ppermute | solution.py:314
  58.5 4.4 %collective-permute-start.6 = (f32[16,1024]{1,0:T(8,128)S(1)}, f32[16,1024]{1,0:T(8,128)S(1)}, u32[]{:S(2)}, u32[]{:S(2)}) collective-permute-start(f32[16,1024]{1,0:T(8,128)S(1)} %multiply_add_fusion.1), channel_id=1, source_target_pairs={{0,4},{1,5},{2,6},{3,7},{4,8},{5,9},{6,10},{7,11},{8,12},{9,13},{1... | collective-permute-start | bytes 196616 | tf_op jit(solution)/shard_map/ppermute | solution.py:314
  63.0 4.6 %collective-permute-start.10 = (f32[16,1024]{1,0:T(8,128)S(1)}, f32[16,1024]{1,0:T(8,128)S(1)}, u32[]{:S(2)}, u32[]{:S(2)}) collective-permute-start(f32[16,1024]{1,0:T(8,128)S(1)} %select_add_fusion.2), channel_id=1, source_target_pairs={{0,2},{1,3},{2,0},{3,1},{4,6},{5,7},{6,4},{7,5},{8,10},{9,11},{10,... | collective-permute-start | bytes 196616 | tf_op jit(solution)/shard_map/ppermute | solution.py:308
  64.1 4.4 %collective-permute-start.9 = (f32[16,1024]{1,0:T(8,128)S(1)}, f32[16,1024]{1,0:T(8,128)S(1)}, u32[]{:S(2)}, u32[]{:S(2)}) collective-permute-start(f32[16,1024]{1,0:T(8,128)S(1)} %select_add_fusion.3), channel_id=1, source_target_pairs={{0,3},{1,2},{2,1},{3,0},{4,7},{5,6},{6,5},{7,4},{8,11},{9,10},{10,... | collective-permute-start | bytes 196616 | tf_op jit(solution)/shard_map/ppermute | solution.py:308
  64.2 4.3 %collective-permute-start.11 = (f32[16,1024]{1,0:T(8,128)S(1)}, f32[16,1024]{1,0:T(8,128)S(1)}, u32[]{:S(2)}, u32[]{:S(2)}) collective-permute-start(f32[16,1024]{1,0:T(8,128)S(1)} %get-tuple-element.15), channel_id=1, source_target_pairs={{0,1},{1,0},{2,3},{3,2},{4,5},{5,4},{6,7},{7,6},{8,9},{9,8},{10,11... | collective-permute-start | bytes 196616 | tf_op jit(solution)/shard_map/ppermute | solution.py:308
  68.6 2.2 %copy-start.3 = (f32[32,8,4096]{2,1,0:T(8,128)S(1)}, f32[32,8,4096]{2,1,0:T(8,128)}, u32[]{:S(2)}) copy-start(f32[32,8,4096]{2,1,0:T(8,128)} %copy-done.2) | copy-start | bytes 12582916
  70.8 1.6 copy-start.9
  72.4 1.6 copy-start.11
  82.0 56.8 %copy-start = (bf16[256,4096]{1,0:T(8,128)(2,1)}, bf16[256,4096]{1,0:T(8,128)(2,1)S(1)}, u32[]{:S(2)}) copy-start(bf16[256,4096]{1,0:T(8,128)(2,1)S(1)} %gate_pass.1.refs_4_.refs_2_) | copy-start | bytes 6291460
  82.0 47.8 %collective-permute-start.13 = (bf16[256,4096]{1,0:T(8,128)(2,1)S(1)}, bf16[256,4096]{1,0:T(8,128)(2,1)}, u32[]{:S(2)}, u32[]{:S(2)}) collective-permute-start(bf16[256,4096]{1,0:T(8,128)(2,1)S(1)} %gate_pass.1.refs_4_.refs_2_), channel_id=1, source_target_pairs={{0,2},{1,3},{2,0},{3,1},{4,6},{5,7},{6,4},{7,5},{8,10},{9,11},{10,... | collective-permute-start | bytes 6291464 | tf_op jit(solution)/shard_map/ppermute | solution.py:308
  83.2 50.2 %collective-permute-start.20 = (bf16[256,4096]{1,0:T(8,128)(2,1)}, bf16[256,4096]{1,0:T(8,128)(2,1)}, u32[]{:S(2)}, u32[]{:S(2)}) collective-permute-start(bf16[256,4096]{1,0:T(8,128)(2,1)} %collective-permute-done.1.refs_3_), channel_id=1, source_target_pairs={{8,4},{9,5},{10,6},{11,7},{4,0},{5,1},{6,2},{7,3},{24,20},{25,21},... | collective-permute-start | bytes 6291464 | tf_op jit(solution)/shard_map/ppermute | solution.py:371
  84.5 50.2 %collective-permute-start.19 = (bf16[256,4096]{1,0:T(8,128)(2,1)}, bf16[256,4096]{1,0:T(8,128)(2,1)}, u32[]{:S(2)}, u32[]{:S(2)}) collective-permute-start(bf16[256,4096]{1,0:T(8,128)(2,1)} %collective-permute-done.refs_2_), channel_id=1, source_target_pairs={{4,8},{5,9},{6,10},{7,11},{8,12},{9,13},{10,14},{11,15},{20,24},{2... | collective-permute-start | bytes 6291464 | tf_op jit(solution)/shard_map/ppermute | solution.py:371
  86.5 52.3 %collective-permute-start.12 = (bf16[256,4096]{1,0:T(8,128)(2,1)S(1)}, bf16[256,4096]{1,0:T(8,128)(2,1)}, u32[]{:S(2)}, u32[]{:S(2)}) collective-permute-start(bf16[256,4096]{1,0:T(8,128)(2,1)S(1)} %gate_pass.1.refs_4_.refs_2_), channel_id=1, source_target_pairs={{0,1},{1,0},{2,3},{3,2},{4,5},{5,4},{6,7},{7,6},{8,9},{9,8},{10,11... | collective-permute-start | bytes 6291464 | tf_op jit(solution)/shard_map/ppermute | solution.py:308
  129.8 8.9 %collective-permute-start.14 = (bf16[256,4096]{1,0:T(8,128)(2,1)}, bf16[256,4096]{1,0:T(8,128)(2,1)}, u32[]{:S(2)}, u32[]{:S(2)}) collective-permute-start(bf16[256,4096]{1,0:T(8,128)(2,1)} %collective-permute-done.13.refs_6_.refs_4_), channel_id=1, source_target_pairs={{0,1},{1,0},{2,3},{3,2},{4,5},{5,4},{6,7},{7,6},{8,9},{9,8},{10,11... | collective-permute-start | bytes 6291464 | tf_op jit(solution)/shard_map/ppermute | solution.py:308
  133.4 49.0 %collective-permute-start.25 = (bf16[256,4096]{1,0:T(8,128)(2,1)}, bf16[256,4096]{1,0:T(8,128)(2,1)}, u32[]{:S(2)}, u32[]{:S(2)}) collective-permute-start(bf16[256,4096]{1,0:T(8,128)(2,1)} %collective-permute-done.20.refs_1_), channel_id=1, source_target_pairs={{4,0},{5,1},{6,2},{7,3},{20,16},{21,17},{22,18},{23,19}} | collective-permute-start | bytes 6291464 | tf_op jit(solution)/shard_map/ppermute | solution.py:371
  134.7 47.7 %collective-permute-start.26 = (bf16[256,4096]{1,0:T(8,128)(2,1)}, bf16[256,4096]{1,0:T(8,128)(2,1)}, u32[]{:S(2)}, u32[]{:S(2)}) collective-permute-start(bf16[256,4096]{1,0:T(8,128)(2,1)} %collective-permute-done.19.refs_0_), channel_id=1, source_target_pairs={{8,12},{9,13},{10,14},{11,15},{24,28},{25,29},{26,30},{27,31}} | collective-permute-start | bytes 6291464 | tf_op jit(solution)/shard_map/ppermute | solution.py:371
  136.8 2.2 %copy-start.1 = (bf16[256,4096]{1,0:T(8,128)(2,1)S(1)}, bf16[256,4096]{1,0:T(8,128)(2,1)}, u32[]{:S(2)}) copy-start(bf16[256,4096]{1,0:T(8,128)(2,1)} %refs_1_.1) | copy-start | bytes 6291460
  148.4 46.7 %collective-permute-start.15 = (bf16[4,512,256]{2,1,0:T(8,128)(2,1)S(1)}, bf16[4,512,256]{2,1,0:T(8,128)(2,1)S(1)}, u32[]{:S(2)}, u32[]{:S(2)}) collective-permute-start(bf16[4,512,256]{2,1,0:T(8,128)(2,1)S(1)} %project.3), channel_id=1, source_target_pairs={{16,0},{17,1},{18,2},{19,3},{20,4},{21,5},{22,6},{23,7},{8,24},{9,... | collective-permute-start | bytes 3145736 | tf_op jit(solution)/shard_map/ppermute | solution.py:390
  156.2 37.4 %collective-permute-start.21 = (bf16[4,256,256]{2,1,0:T(8,128)(2,1)S(1)}, bf16[4,256,256]{2,1,0:T(8,128)(2,1)S(1)}, u32[]{:S(2)}, u32[]{:S(2)}) collective-permute-start(bf16[4,256,256]{2,1,0:T(8,128)(2,1)S(1)} %project.4), channel_id=1, source_target_pairs={{0,16},{1,17},{2,18},{3,19},{4,20},{5,21},{6,22},{7,23},{24,8},{25... | collective-permute-start | bytes 1572872 | tf_op jit(solution)/shard_map/ppermute | solution.py:390
  190.1 13.1 %collective-permute-start.27 = (bf16[4,256,256]{2,1,0:T(8,128)(2,1)S(1)}, bf16[4,256,256]{2,1,0:T(8,128)(2,1)S(1)}, u32[]{:S(2)}, u32[]{:S(2)}) collective-permute-start(bf16[4,256,256]{2,1,0:T(8,128)(2,1)S(1)} %project.5), channel_id=1, source_target_pairs={{0,16},{1,17},{2,18},{3,19},{4,20},{5,21},{6,22},{7,23},{24,8},{25... | collective-permute-start | bytes 1572872 | tf_op jit(solution)/shard_map/ppermute | solution.py:390
  194.4 4.9 %collective-permute-start.22 = (bf16[256,256]{1,0:T(8,128)(2,1)S(1)}, bf16[256,256]{1,0:T(8,128)(2,1)S(1)}, u32[]{:S(2)}, u32[]{:S(2)}) collective-permute-start(bf16[256,256]{1,0:T(8,128)(2,1)S(1)} %get-tuple-element.27), channel_id=1, source_target_pairs={{16,17},{17,16},{18,19},{19,18},{20,21},{21,20},{22,23},{23,22},{8... | collective-permute-start | bytes 393224 | tf_op jit(solution)/shard_map/ppermute | solution.py:399
  196.0 11.3 %collective-permute-start.16 = (bf16[512,256]{1,0:T(8,128)(2,1)S(1)}, bf16[512,256]{1,0:T(8,128)(2,1)S(1)}, u32[]{:S(2)}, u32[]{:S(2)}) collective-permute-start(bf16[512,256]{1,0:T(8,128)(2,1)S(1)} %get-tuple-element.19), channel_id=1, source_target_pairs={{0,1},{1,0},{2,3},{3,2},{4,5},{5,4},{6,7},{7,6},{24,25},{25,24},{2... | collective-permute-start | bytes 786440 | tf_op jit(solution)/shard_map/ppermute | solution.py:399
  197.9 8.0 %collective-permute-start.23 = (bf16[256,256]{1,0:T(8,128)(2,1)S(1)}, bf16[256,256]{1,0:T(8,128)(2,1)S(1)}, u32[]{:S(2)}, u32[]{:S(2)}) collective-permute-start(bf16[256,256]{1,0:T(8,128)(2,1)S(1)} %get-tuple-element.26), channel_id=1, source_target_pairs={{16,18},{17,19},{18,16},{19,17},{20,22},{21,23},{22,20},{23,21},{8... | collective-permute-start | bytes 393224 | tf_op jit(solution)/shard_map/ppermute | solution.py:399
  198.6 8.0 %collective-permute-start.24 = (bf16[256,256]{1,0:T(8,128)(2,1)S(1)}, bf16[256,256]{1,0:T(8,128)(2,1)S(1)}, u32[]{:S(2)}, u32[]{:S(2)}) collective-permute-start(bf16[256,256]{1,0:T(8,128)(2,1)S(1)} %get-tuple-element.25), channel_id=1, source_target_pairs={{16,19},{17,18},{18,17},{19,16},{20,23},{21,22},{22,21},{23,20},{8... | collective-permute-start | bytes 393224 | tf_op jit(solution)/shard_map/ppermute | solution.py:399
  199.3 15.9 %copy-start.16 = (bf16[256,256]{1,0:T(8,128)(2,1)}, bf16[256,256]{1,0:T(8,128)(2,1)S(1)}, u32[]{:S(2)}) copy-start(bf16[256,256]{1,0:T(8,128)(2,1)S(1)} %collective-permute-done.22.refs_5_) | copy-start | bytes 393220
  199.3 11.0 %collective-permute-start.17 = (bf16[512,256]{1,0:T(8,128)(2,1)S(1)}, bf16[512,256]{1,0:T(8,128)(2,1)S(1)}, u32[]{:S(2)}, u32[]{:S(2)}) collective-permute-start(bf16[512,256]{1,0:T(8,128)(2,1)S(1)} %get-tuple-element.18), channel_id=1, source_target_pairs={{0,2},{1,3},{2,0},{3,1},{4,6},{5,7},{6,4},{7,5},{24,26},{25,27},{2... | collective-permute-start | bytes 786440 | tf_op jit(solution)/shard_map/ppermute | solution.py:399
  203.2 11.9 %collective-permute-start.18 = (bf16[512,256]{1,0:T(8,128)(2,1)S(1)}, bf16[512,256]{1,0:T(8,128)(2,1)S(1)}, u32[]{:S(2)}, u32[]{:S(2)}) collective-permute-start(bf16[512,256]{1,0:T(8,128)(2,1)S(1)} %get-tuple-element.17), channel_id=1, source_target_pairs={{0,3},{1,2},{2,1},{3,0},{4,7},{5,6},{6,5},{7,4},{24,27},{25,26},{2... | collective-permute-start | bytes 786440 | tf_op jit(solution)/shard_map/ppermute | solution.py:399
  205.9 9.3 %copy-start.17 = (bf16[256,256]{1,0:T(8,128)(2,1)}, bf16[256,256]{1,0:T(8,128)(2,1)S(1)}, u32[]{:S(2)}) copy-start(bf16[256,256]{1,0:T(8,128)(2,1)S(1)} %collective-permute-done.23.refs_6_) | copy-start | bytes 393220
  205.9 9.2 %collective-permute-start.28 = (bf16[256,256]{1,0:T(8,128)(2,1)S(1)}, bf16[256,256]{1,0:T(8,128)(2,1)S(1)}, u32[]{:S(2)}, u32[]{:S(2)}) collective-permute-start(bf16[256,256]{1,0:T(8,128)(2,1)S(1)} %get-tuple-element.23), channel_id=1, source_target_pairs={{16,17},{17,16},{18,19},{19,18},{20,21},{21,20},{22,23},{23,22},{8... | collective-permute-start | bytes 393224 | tf_op jit(solution)/shard_map/ppermute | solution.py:399
  206.6 8.6 %copy-start.18 = (bf16[256,256]{1,0:T(8,128)(2,1)}, bf16[256,256]{1,0:T(8,128)(2,1)S(1)}, u32[]{:S(2)}) copy-start(bf16[256,256]{1,0:T(8,128)(2,1)S(1)} %collective-permute-done.24.refs_7_) | copy-start | bytes 393220
  206.6 8.5 %collective-permute-start.29 = (bf16[256,256]{1,0:T(8,128)(2,1)S(1)}, bf16[256,256]{1,0:T(8,128)(2,1)S(1)}, u32[]{:S(2)}, u32[]{:S(2)}) collective-permute-start(bf16[256,256]{1,0:T(8,128)(2,1)S(1)} %get-tuple-element.22), channel_id=1, source_target_pairs={{16,18},{17,19},{18,16},{19,17},{20,22},{21,23},{22,20},{23,21},{8... | collective-permute-start | bytes 393224 | tf_op jit(solution)/shard_map/ppermute | solution.py:399
  207.3 7.9 %copy-start.13 = (bf16[512,256]{1,0:T(8,128)(2,1)}, bf16[512,256]{1,0:T(8,128)(2,1)S(1)}, u32[]{:S(2)}) copy-start(bf16[512,256]{1,0:T(8,128)(2,1)S(1)} %collective-permute-done.16.refs_1_) | copy-start | bytes 786436
  207.3 7.8 %collective-permute-start.30 = (bf16[256,256]{1,0:T(8,128)(2,1)S(1)}, bf16[256,256]{1,0:T(8,128)(2,1)S(1)}, u32[]{:S(2)}, u32[]{:S(2)}) collective-permute-start(bf16[256,256]{1,0:T(8,128)(2,1)S(1)} %get-tuple-element.21), channel_id=1, source_target_pairs={{16,19},{17,18},{18,17},{19,16},{20,23},{21,22},{22,21},{23,20},{8... | collective-permute-start | bytes 393224 | tf_op jit(solution)/shard_map/ppermute | solution.py:399
  210.3 4.9 %copy-start.14 = (bf16[512,256]{1,0:T(8,128)(2,1)}, bf16[512,256]{1,0:T(8,128)(2,1)S(1)}, u32[]{:S(2)}) copy-start(bf16[512,256]{1,0:T(8,128)(2,1)S(1)} %collective-permute-done.17.refs_2_) | copy-start | bytes 786436
  (5 other events, 4.4 us)
